TPU v7x, 32 devices: a whole 2x2x4 slice. The times are simulated.
32 devices in a mesh: groups: 2 (over y), team: 4 (over z), rep: 4 (over x, core).
Axes of the slice: x: 2, y: 2, z: 4, core: 2. Of those that a mesh axis runs over, the one named last changes fastest.
Arguments:
- omega_rows: float32 [128, 32768], P(('groups', 'team'), 'rep'), parts along dimension 0, as said below
- covariance_columns: float32 [32768, 2048], P('rep', ('groups', 'team')), parts along dimension 1, may hold values from -0.03125 to 0.03125
- tile_offsets: int32 [8], P(('groups', 'team')), parts along dimension 0, may hold values from 0 to 32512, as said below
Outputs:
- new_omega: float32 [64, 2048], P('rep', ('groups', 'team')), parts along dimension 1
There are 2 independent parts, one for each index of `groups`. A program takes and returns all parts, laid end to end along the dimension named above; each array names one. Nothing has to cross between parts.
Inputs may be any that keep to these rules, and one draw needn't show every extreme that they name: `tile_offsets`: distinct multiples of 256; both 0 and 32512 occur. `omega_rows`: entries with column equal to row lie in 1 to 2.
All inputs are finite; a program needn't handle non-finite values.
Results may differ from a plain program's by a relative error of at most 0.0003.
Values sent between devices are 32-bit elements; how exact they have to be, the bound alone decides.
A program may use at most 64 MiB of HBM per device.

v0:
```python
import jax
import jax.numpy as jnp
from jax import lax
from jax.sharding import PartitionSpec as P

step_size = 0.5
penalty = 0.1


def shifted(array, axis, by):
    devices = lax.axis_size(axis)
    return lax.ppermute(array, axis, [(i, (i + by) % devices) for i in range(devices)])


def from_root(array, axis, root):
    mine = lax.axis_index(axis) == root
    return lax.psum(jnp.where(mine, array, jnp.zeros_like(array)), axis)


def per_device(omega_rows, covariance_columns, tile_offsets):
    team_count = lax.axis_size("team")
    rep_count = lax.axis_size("rep")
    team_index = lax.axis_index("team")
    rep_index = lax.axis_index("rep")
    block_rows, part_width = omega_rows.shape
    tile_width = covariance_columns.shape[1]
    all_rows = block_rows * team_count
    rows_share = all_rows // rep_count
    offset = tile_offsets[0]
    owner = offset // part_width
    inside = jnp.clip(offset - rep_index * part_width, 0, part_width - tile_width)

    def place(collected, block, source):
        first = source * block_rows
        return lax.dynamic_update_slice_in_dim(collected, block, first, 0)

    empty = jnp.zeros((all_rows, part_width), jnp.float32)

    def advance(shift_count, carry):
        block, collected = carry
        block = shifted(block, "team", 1)
        source = (team_index - shift_count) % team_count
        return (block, place(collected, block, source))

    final = lax.fori_loop(
        1, team_count, advance, (omega_rows, place(empty, omega_rows, team_index))
    )
    collected = final[1]
    partial_value = jnp.dot(
        collected,
        covariance_columns,
        preferred_element_type=jnp.float32,
        precision=lax.Precision.HIGHEST,
    )
    values = lax.dynamic_slice_in_dim(collected, inside, tile_width, 1)
    summed = lax.psum_scatter(partial_value, "rep", scatter_dimension=0, tiled=True)
    everyone = from_root(values, "rep", owner)
    current = lax.dynamic_slice_in_dim(everyone, rep_index * rows_share, rows_share, 0)
    global_rows = rep_index * rows_share + jnp.arange(rows_share, dtype=jnp.int32)
    global_cols = offset + jnp.arange(tile_width, dtype=jnp.int32)
    diagonal = global_rows[:, None] == global_cols[None, :]
    safe = jnp.where(diagonal, current, jnp.float32(1.0))
    gradient = summed - jnp.where(diagonal, 1.0 / safe, jnp.float32(0.0))
    moved = current - step_size * gradient
    shrunk = jnp.sign(moved) * jnp.maximum(jnp.abs(moved) - step_size * penalty, 0.0)
    return jnp.where(diagonal, moved, shrunk)


def solution(mesh):
    in_specs = (P(("groups", "team"), "rep"), P("rep", ("groups", "team")), P(("groups", "team")))
    out_specs = P("rep", ("groups", "team"))
    return jax.shard_map(
        per_device, mesh=mesh, in_specs=in_specs, out_specs=out_specs, check_vma=False
    )
```

profile of v0, /device:TPU:0, one launch (start us, length us, event | category | flops | bytes accessed | tf_op | source)
XLA Modules:
  0.0 114.8 jit_solution(6271310564918737601)
XLA Ops:
  6.5 0.0 all-reduce.2.cloned.1.call-start
  6.5 1.0 copy.18
  8.3 0.1 broadcast_in_dim.13
  8.5 46.3 %while.17 = (s32[]{:T(128)}, f32[16,8192]{1,0:T(8,128)S(1)}, f32[64,8192]{1,0:T(8,128)S(1)}, s32[]{:T(128)}, s32[]{:T(128)}, /*index=5*/s32[]{:T(128)}, s32[]{:T(128)}, s32[]{:T(128)}, s32[]{:T(128)}, s32[]{:T(128)}) while((s32[]{:T(128)}, f32[16,8192]{1,0:T(8,128)S(1)}, f32[64,8192]{1,0:T(8,128)S(1)}, s32[]{:T(128)}, s32[]{:T(128)}, ...), condition=%wide.region_1.2_spmd, body=%wide.region_0.1_spmd.sunk | while | flops 18 | bytes 4194616 | solution.py:45
  8.5 3.1 %collective-permute-start = (f32[16,8192]{1,0:T(8,128)S(1)}, f32[16,8192]{1,0:T(8,128)S(1)}, u32[]{:S(2)}, u32[]{:S(2)}) collective-permute-start(f32[16,8192]{1,0:T(8,128)S(1)} %get-tuple-element.161), channel_id=1, source_target_pairs={{0,4},{4,8},{8,12},{12,0},{1,5},{5,9},{9,13},{13,1},{2,6},{6,10},{... | collective-permute-start | bytes 1572872 | tf_op jit(solution)/shard_map/while/body/eval_jaxpr/ppermute | solution.py:12
  11.5 13.9 %collective-permute-done = f32[16,8192]{1,0:T(8,128)S(1)} collective-permute-done((f32[16,8192]{1,0:T(8,128)S(1)}, f32[16,8192]{1,0:T(8,128)S(1)}, u32[]{:S(2)}, u32[]{:S(2)}) %collective-permute-start) | collective-permute-done | bytes 524320 | tf_op jit(solution)/shard_map/while/body/eval_jaxpr/ppermute | solution.py:12
  25.6 0.1 collective-permute-start
  25.7 14.9 %collective-permute-done = f32[16,8192]{1,0:T(8,128)S(1)} collective-permute-done((f32[16,8192]{1,0:T(8,128)S(1)}, f32[16,8192]{1,0:T(8,128)S(1)}, u32[]{:S(2)}, u32[]{:S(2)}) %collective-permute-start) | collective-permute-done | bytes 524320 | tf_op jit(solution)/shard_map/while/body/eval_jaxpr/ppermute | solution.py:12
  40.7 0.1 collective-permute-start
  40.7 13.9 %collective-permute-done = f32[16,8192]{1,0:T(8,128)S(1)} collective-permute-done((f32[16,8192]{1,0:T(8,128)S(1)}, f32[16,8192]{1,0:T(8,128)S(1)}, u32[]{:S(2)}, u32[]{:S(2)}) %collective-permute-start) | collective-permute-done | bytes 524320 | tf_op jit(solution)/shard_map/while/body/eval_jaxpr/ppermute | solution.py:12
  54.8 0.7 dynamic-slice_select_fusion
  55.5 0.0 all-reduce.2.cloned.1.call-update
  55.5 0.0 reduce-scatter.2.cloned.1.call-start
  55.6 7.3 %fusion.4 = f32[64,256]{1,0:T(8,128)} fusion(f32[64,8192]{1,0:T(8,128)S(1)} %get-tuple-element.116, f32[8192,256]{1,0:T(8,128)} %param.6), kind=kOutput, calls=%fused_computation.12 | convolution fusion | flops 1610612736 | bytes 10551296 | tf_op jit(solution)/shard_map/dot_general | solution.py:49
  62.9 0.0 reduce-scatter.2.cloned.1.call-update
  63.0 21.5 %all-reduce.2.cloned.1.call-done = f32[64,256]{1,0:T(8,128)} async-done(((f32[64,256]{1,0:T(8,128)}), f32[64,256]{1,0:T(8,128)}) %all-reduce.2.cloned.1.call-update) | async-done | bytes 65552 | tf_op jit(solution)/shard_map/psum | solution.py:17
  84.5 22.0 %reduce-scatter.2.cloned.1.call-done = f32[16,256]{1,0:T(8,128)} async-done(((f32[64,256]{1,0:T(8,128)}), f32[16,256]{1,0:T(8,128)}) %reduce-scatter.2.cloned.1.call-update) | async-done | bytes 16400 | tf_op jit(solution)/shard_map/reduce_scatter | solution.py:56
  106.5 1.4 %compare_select_fusion = f32[16,256]{1,0:T(8,128)} fusion(f32[16,256]{1,0:T(8,128)} %reduce-scatter.2.cloned.1.call-done, f32[64,256]{1,0:T(8,128)} %all-reduce.2.cloned.1.call-done, s32[]{:T(128)S(6)} %select_n.64, s32[256]{0:T(256)S(1)} %iota_add_fusion, s32[16]{0:T(128)S(1)} %iota_add_fusion.1), kind=kLoop, calls=%fused_computation.2 | loop fusion | flops 53248 | bytes 50244 | tf_op jit(solution)/shard_map/jit(_where)/select_n | solution.py:66
  (9 shorter events, 0.3 us)
Async XLA Ops:
  6.5 78.0 %all-reduce.2.cloned.1.call-start = ((), (), s32[]{:S(2)}) async-start(), calls=%async_computation.1 | async-start | bytes 131072 | tf_op jit(solution)/shard_map/psum | solution.py:17
  8.5 17.0 %collective-permute-start = (f32[16,8192]{1,0:T(8,128)S(1)}, f32[16,8192]{1,0:T(8,128)S(1)}, u32[]{:S(2)}, u32[]{:S(2)}) collective-permute-start(f32[16,8192]{1,0:T(8,128)S(1)} %get-tuple-element.161), channel_id=1, source_target_pairs={{0,4},{4,8},{8,12},{12,0},{1,5},{5,9},{9,13},{13,1},{2,6},{6,10},{... | collective-permute-start | bytes 1572872 | tf_op jit(solution)/shard_map/while/body/eval_jaxpr/ppermute | solution.py:12
  25.6 15.0 %collective-permute-start = (f32[16,8192]{1,0:T(8,128)S(1)}, f32[16,8192]{1,0:T(8,128)S(1)}, u32[]{:S(2)}, u32[]{:S(2)}) collective-permute-start(f32[16,8192]{1,0:T(8,128)S(1)} %get-tuple-element.161), channel_id=1, source_target_pairs={{0,4},{4,8},{8,12},{12,0},{1,5},{5,9},{9,13},{13,1},{2,6},{6,10},{... | collective-permute-start | bytes 1572872 | tf_op jit(solution)/shard_map/while/body/eval_jaxpr/ppermute | solution.py:12
  40.7 14.0 %collective-permute-start = (f32[16,8192]{1,0:T(8,128)S(1)}, f32[16,8192]{1,0:T(8,128)S(1)}, u32[]{:S(2)}, u32[]{:S(2)}) collective-permute-start(f32[16,8192]{1,0:T(8,128)S(1)} %get-tuple-element.161), channel_id=1, source_target_pairs={{0,4},{4,8},{8,12},{12,0},{1,5},{5,9},{9,13},{13,1},{2,6},{6,10},{... | collective-permute-start | bytes 1572872 | tf_op jit(solution)/shard_map/while/body/eval_jaxpr/ppermute | solution.py:12
  55.5 51.0 %reduce-scatter.2.cloned.1.call-start = ((), (), s32[]{:S(2)}) async-start(), calls=%async_computation.2 | async-start | bytes 81920 | tf_op jit(solution)/shard_map/reduce_scatter | solution.py:56
Sparse Core Ops, SparseCore 0:
  55.7 28.7 all-reduce.1
  87.0 19.4 reduce-scatter.1
where the time goes:
time: 115 us
  waiting for transfers between devices  86.4 us (75%)
  between operations  14.1 us (12%)
  matrix products  7.33 us (6%)
  starting transfers between devices  3.24 us (3%)
  other arithmetic  2.16 us (2%)
  local copies, waits for them, and re-layouts  1.45 us (1%)
    ppermute x3, waiting for transfers between devices, shifted(): lax.ppermute(array, axis, [(i, (i + by) % devices) for i in range(devices)])  42.8 us
    reduce_scatter x1, waiting for transfers between devices, per_device(): lax.psum_scatter(partial_value, 'rep', scatter_dimension=0, tiled=True)  22 us
    psum x1, waiting for transfers between devices, from_root(): return lax.psum(jnp.where(mine, array, jnp.zeros_like(array)), axis)  21.5 us
    dot_general x1, matrix products, per_device(): jnp.dot(collected, covariance_columns, preferred_element_type=jnp.float32...  7.33 us
    ppermute x3, starting transfers between devices, shifted(): lax.ppermute(array, axis, [(i, (i + by) % devices) for i in range(devices)])  3.19 us
  transfers between devices with their start and end apart: 5, of which 5 were waited for; matrix products, arithmetic and copies ran while one was open for 6% of the time, Pallas kernels for 0%

commit v1 on v0

v1 whole, which is shorter than its diff:
```python
import functools

import jax
import jax.numpy as jnp
from jax import lax
from jax.experimental import pallas as pl
from jax.experimental.pallas import tpu as pltpu
from jax.sharding import PartitionSpec as P

MESH = pl.DeviceIdType.MESH
step_size = 0.5
penalty = 0.1


def kernel(teams, reps, chunks, omega, cov, offset, out, gath, stage, high, low, acc,
           current, part, inbox, cov_sem, own_sem, right_send, right_recv, left_send, left_recv, sum_send,
           sum_recv):
    t = lax.axis_index("team")
    r = lax.axis_index("rep")
    rows, width = omega.shape
    tile = cov.shape[1]
    piece = width // chunks
    share = teams * rows // reps

    def span(c):
        return pl.ds(pl.multiple_of(c * piece, piece), piece)

    def cov_copy(c):
        return pltpu.make_async_copy(cov.at[span(c), :], stage.at[span(c), :], cov_sem.at[c])

    own_copy = pltpu.make_async_copy(omega, gath.at[t], own_sem)
    own_copy.start()
    for c in range(chunks):
        cov_copy(c).start()

    barrier = pltpu.get_barrier_semaphore()

    @pl.when(t > 0)
    def _():
        pl.semaphore_signal(barrier, inc=1, device_id={"team": t - 1}, device_id_type=MESH)

    @pl.when(t < teams - 1)
    def _():
        pl.semaphore_signal(barrier, inc=1, device_id={"team": t + 1}, device_id_type=MESH)

    for d in range(1, reps):
        peer = lax.rem(r + d, reps)
        pl.semaphore_signal(barrier, inc=1, device_id={"rep": peer}, device_id_type=MESH)

    sides = jnp.where(t > 0, 1, 0) + jnp.where(t < teams - 1, 1, 0)
    pl.semaphore_wait(barrier, reps - 1 + sides)

    def send(way, q, own):
        block = t - (q // chunks) * way
        c = lax.rem(q, chunks)
        sems = (right_send, right_recv) if way > 0 else (left_send, left_recv)
        source = omega.at[:, span(c)] if own else gath.at[block, :, span(c)]
        return pltpu.make_async_remote_copy(
            src_ref=source, dst_ref=gath.at[block, :, span(c)],
            send_sem=sems[0].at[q], recv_sem=sems[1].at[q],
            device_id={"team": t + way}, device_id_type=MESH)

    def arrival(way, q):
        block = t - (q // chunks + 1) * way
        c = lax.rem(q, chunks)
        sems = (right_send, right_recv) if way > 0 else (left_send, left_recv)
        return pltpu.make_async_remote_copy(
            src_ref=gath.at[block, :, span(c)], dst_ref=gath.at[block, :, span(c)],
            send_sem=sems[0].at[q], recv_sem=sems[1].at[q],
            device_id={"team": t - way}, device_id_type=MESH)

    for c in range(chunks):
        @pl.when(t < teams - 1)
        def _():
            send(1, jnp.int32(c), True).start()

        @pl.when(t > 0)
        def _():
            send(-1, jnp.int32(c), True).start()

    acc[...] = jnp.zeros_like(acc)
    current[...] = jnp.zeros_like(current)
    origin = offset[0]

    def multiply(block, c):
        a = gath[block, :, span(c)]
        a_high = a.astype(jnp.bfloat16)
        a_low = (a - a_high.astype(jnp.float32)).astype(jnp.bfloat16)
        both = jnp.concatenate([a_high, a_low], axis=0)
        first = jnp.dot(both, high[span(c), :], preferred_element_type=jnp.float32)
        second = jnp.dot(both, low[span(c), :], preferred_element_type=jnp.float32)
        whole = first + second
        acc[pl.ds(pl.multiple_of(block * rows, rows), rows), :] += whole[:rows] + whole[rows:]
        found = jnp.zeros((rows, tile), jnp.float32)
        for k in range(piece // tile):
            begin = jnp.full((rows, tile), r * width + c * piece + k * tile, jnp.int32)
            found = found + jnp.where(begin == origin, a[:, k * tile:(k + 1) * tile], 0.0)
        current[pl.ds(pl.multiple_of(block * rows, rows), rows), :] += found

    own_copy.wait()

    @pl.loop(0, chunks)
    def _(c):
        cov_copy(c).wait()
        value = stage[span(c), :]
        top = value.astype(jnp.bfloat16)
        high[span(c), :] = top
        low[span(c), :] = (value - top.astype(jnp.float32)).astype(jnp.bfloat16)
        multiply(t, c)

    @pl.loop(0, (teams - 1) * chunks)
    def _(q):
        has_left = q < t * chunks
        has_right = q < (teams - 1 - t) * chunks

        @pl.when(has_left)
        def _():
            arrival(1, q).wait_recv()

            @pl.when(t < teams - 1)
            def _():
                send(1, q + chunks, False).start()

        @pl.when(has_right)
        def _():
            arrival(-1, q).wait_recv()

            @pl.when(t > 0)
            def _():
                send(-1, q + chunks, False).start()

        @pl.when(has_left)
        def _():
            multiply(t - 1 - q // chunks, lax.rem(q, chunks))

        @pl.when(has_right)
        def _():
            multiply(t + 1 + q // chunks, lax.rem(q, chunks))

    for s in range(teams):
        values = current[s * rows:(s + 1) * rows, :]
        row_ids = s * rows + lax.broadcasted_iota(jnp.int32, (rows, tile), 0)
        col_ids = origin + lax.broadcasted_iota(jnp.int32, (rows, tile), 1)
        mine = jnp.logical_and(col_ids >= r * width, col_ids < (r + 1) * width)
        diagonal = jnp.logical_and(row_ids == col_ids, mine)
        safe = jnp.where(diagonal, values, 1.0)
        kept = values + jnp.where(diagonal, step_size / safe, 0.0)
        part[s * rows:(s + 1) * rows, :] = kept - step_size * acc[s * rows:(s + 1) * rows, :]

    def exchange(d):
        peer = lax.rem(r + d, reps)
        return pltpu.make_async_remote_copy(
            src_ref=part.at[pl.ds(pl.multiple_of(peer * share, share), share), :],
            dst_ref=inbox.at[d - 1], send_sem=sum_send.at[d - 1], recv_sem=sum_recv.at[d - 1],
            device_id={"rep": peer}, device_id_type=MESH)

    for d in range(1, reps):
        exchange(d).start()
    total = part[pl.ds(pl.multiple_of(r * share, share), share), :]
    for d in range(1, reps):
        exchange(d).wait_recv()
        total = total + inbox[d - 1]
    out[...] = total

    for d in range(1, reps):
        exchange(d).wait_send()

    @pl.loop(0, teams * chunks)
    def _(q):
        @pl.when(jnp.logical_and(t < teams - 1, q < (t + 1) * chunks))
        def _():
            send(1, q, False).wait_send()

        @pl.when(jnp.logical_and(t > 0, q < (teams - t) * chunks))
        def _():
            send(-1, q, False).wait_send()


def per_device(teams, reps, omega_rows, covariance_columns, tile_offsets):
    rows, width = omega_rows.shape
    tile = covariance_columns.shape[1]
    share = rows * teams // reps
    chunks = max(1, min(32 // teams, width // 256))
    dma = pltpu.SemaphoreType.DMA
    moved = pl.pallas_call(
        functools.partial(kernel, teams, reps, chunks),
        out_shape=jax.ShapeDtypeStruct((share, tile), jnp.float32),
        in_specs=[
            pl.BlockSpec(memory_space=pl.ANY),
            pl.BlockSpec(memory_space=pl.ANY),
            pl.BlockSpec(memory_space=pltpu.SMEM),
        ],
        out_specs=pl.BlockSpec(memory_space=pltpu.VMEM),
        scratch_shapes=[
            pltpu.VMEM((teams, rows, width), jnp.float32),
            pltpu.VMEM((width, tile), jnp.float32),
            pltpu.VMEM((width, tile), jnp.bfloat16),
            pltpu.VMEM((width, tile), jnp.bfloat16),
            pltpu.VMEM((teams * rows, tile), jnp.float32),
            pltpu.VMEM((teams * rows, tile), jnp.float32),
            pltpu.VMEM((teams * rows, tile), jnp.float32),
            pltpu.VMEM((reps - 1, share, tile), jnp.float32),
            dma((chunks,)),
            dma,
            dma((teams * chunks,)),
            dma((teams * chunks,)),
            dma((teams * chunks,)),
            dma((teams * chunks,)),
            dma((reps - 1,)),
            dma((reps - 1,)),
        ],
        compiler_params=pltpu.CompilerParams(
            collective_id=0, has_side_effects=True, vmem_limit_bytes=48 * 1024 * 1024),
        cost_estimate=pl.CostEstimate(
            flops=8 * teams * rows * width * tile,
            bytes_accessed=4 * width * (tile + rows * teams), transcendentals=0),
    )(omega_rows, covariance_columns, tile_offsets)
    global_rows = lax.axis_index("rep") * share + jnp.arange(share, dtype=jnp.int32)
    global_cols = tile_offsets[0] + jnp.arange(tile, dtype=jnp.int32)
    diagonal = global_rows[:, None] == global_cols[None, :]
    shrunk = jnp.sign(moved) * jnp.maximum(jnp.abs(moved) - step_size * penalty, 0.0)
    return jnp.where(diagonal, moved, shrunk)


def solution(mesh):
    in_specs = (P(("groups", "team"), "rep"), P("rep", ("groups", "team")), P(("groups", "team")))
    out_specs = P("rep", ("groups", "team"))
    body = functools.partial(per_device, mesh.shape["team"], mesh.shape["rep"])
    return jax.shard_map(body, mesh=mesh, in_specs=in_specs, out_specs=out_specs, check_vma=False)
```

time: 115 us -> 46.4 us (0.40)
  waiting for transfers between devices: 86.4 us -> 0 us
  Pallas kernels: 0 us -> 43.9 us
  between operations: 14.1 us -> 0.68 us
  matrix products: 7.33 us -> 0 us
  starting transfers between devices: 3.24 us -> 0 us
  other arithmetic: 2.16 us -> 0.69 us
    pallas_call x0 -> x1, Pallas kernels: none -> 43.9 us  [per_device(): pl.pallas_call(functools.partial(kernel, teams, reps, chunks), out_shape=...]
    ppermute x3 -> x0, waiting for transfers between devices: 42.8 us -> none  [shifted(): lax.ppermute(array, axis, [(i, (i + by) % devices) for i in range(devices)])]
    reduce_scatter x1 -> x0, waiting for transfers between devices: 22 us -> none  [per_device(): lax.psum_scatter(partial_value, 'rep', scatter_dimension=0, tiled=True)]
    psum x1 -> x0, waiting for transfers between devices: 21.5 us -> none  [from_root(): return lax.psum(jnp.where(mine, array, jnp.zeros_like(array)), axis)]
    dot_general x1 -> x0, matrix products: 7.33 us -> none  [per_device(): jnp.dot(collected, covariance_columns, preferred_element_type=jnp.float32...]
    ppermute x3 -> x0, starting transfers between devices: 3.19 us -> none  [shifted(): lax.ppermute(array, axis, [(i, (i + by) % devices) for i in range(devices)])]
  transfers between devices with their start and end apart: 5 -> 0, of which waited for: 5 -> 0; matrix products, arithmetic and copies ran while one was open for 6% -> 0% of each run, Pallas kernels for 0% -> 0%
where the time goes in v1:
time: 46.4 us; the launch traced here: 46.3 us
  Pallas kernels  43.9 us (95%)
  local copies, waits for them, and re-layouts  1.04 us (2%)
  other arithmetic  0.69 us (1%)
  between operations  0.68 us (1%)
    pallas_call x1, Pallas kernels, per_device(): pl.pallas_call(functools.partial(kernel, teams, reps, chunks), out_shape=...  43.9 us
    unnamed x2, local copies, waits for them, and re-layouts  1.04 us

profile of v1, /device:TPU:0, one launch (start us, length us, event | category | flops | bytes accessed | tf_op | source)
XLA Modules:
  0.0 46.3 jit_solution(3946109133727816264)
XLA Ops:
  0.7 0.0 copy-start
  0.7 1.0 %copy-done = f32[16,8192]{1,0:T(8,128)S(1)} copy-done((f32[16,8192]{1,0:T(8,128)S(1)}, f32[16,8192]{1,0:T(8,128)}, u32[]{:S(2)}) %copy-start) | copy-done | bytes 524312
  1.7 43.9 %shard_map.37 = f32[16,256]{1,0:T(8,128)S(1)} custom-call(f32[16,8192]{1,0:T(8,128)S(1)} %copy-done, f32[8192,256]{1,0:T(8,128)} %cov.1, s32[1]{0:T(128)} %copy.4.offset), custom_call_target="tpu_custom_call" | custom-call | flops 1073741824 | bytes 10485760 | tf_op jit(solution)/shard_map/pallas_call | solution.py:185
  45.6 0.7 %multiply_select_fusion = f32[16,256]{1,0:T(8,128)} fusion(f32[16,256]{1,0:T(8,128)S(1)} %shard_map.37, s32[256]{0:T(256)S(1)} %iota_add_fusion, s32[16]{0:T(128)S(1)} %iota_add_fusion.1), kind=kLoop, calls=%fused_computation | loop fusion | flops 28672 | bytes 33856 | tf_op jit(solution)/shard_map/jit(_where)/select_n | solution.py:222
  (2 shorter events, 0.0 us)
Async XLA Ops:
  0.7 1.0 %copy-start = (f32[16,8192]{1,0:T(8,128)S(1)}, f32[16,8192]{1,0:T(8,128)}, u32[]{:S(2)}) copy-start(f32[16,8192]{1,0:T(8,128)} %omega.1) | copy-start | bytes 1572868

commit v2 on v1

--- a/solution.py
+++ b/solution.py
@@ -12,9 +12,9 @@
 penalty = 0.1
 
 
-def kernel(teams, reps, chunks, omega, cov, offset, out, gath, stage, high, low, acc,
+def kernel(teams, reps, chunks, window, omega, cov, offset, out, gath, stage, high, low, acc,
            current, part, inbox, cov_sem, own_sem, right_send, right_recv, left_send, left_recv, sum_send,
-           sum_recv):
+           sum_recv, place, place_sem):
     t = lax.axis_index("team")
     r = lax.axis_index("rep")
     rows, width = omega.shape
@@ -30,6 +30,8 @@
 
     own_copy = pltpu.make_async_copy(omega, gath.at[t], own_sem)
     own_copy.start()
+    place_copy = pltpu.make_async_copy(offset, place, place_sem)
+    place_copy.start()
     for c in range(chunks):
         cov_copy(c).start()
 
@@ -69,18 +71,10 @@
             send_sem=sems[0].at[q], recv_sem=sems[1].at[q],
             device_id={"team": t - way}, device_id_type=MESH)
 
-    for c in range(chunks):
-        @pl.when(t < teams - 1)
-        def _():
-            send(1, jnp.int32(c), True).start()
-
-        @pl.when(t > 0)
-        def _():
-            send(-1, jnp.int32(c), True).start()
-
     acc[...] = jnp.zeros_like(acc)
     current[...] = jnp.zeros_like(current)
-    origin = offset[0]
+    place_copy.wait()
+    origin = place[0]
 
     def multiply(block, c):
         a = gath[block, :, span(c)]
@@ -99,43 +93,46 @@
 
     own_copy.wait()
 
-    @pl.loop(0, chunks)
-    def _(c):
-        cov_copy(c).wait()
-        value = stage[span(c), :]
-        top = value.astype(jnp.bfloat16)
-        high[span(c), :] = top
-        low[span(c), :] = (value - top.astype(jnp.float32)).astype(jnp.bfloat16)
-        multiply(t, c)
-
-    @pl.loop(0, (teams - 1) * chunks)
+    def behind(way):
+        return t if way > 0 else teams - 1 - t
+
+    def forward(way, q):
+        sends = jnp.logical_and(behind(-way) > 0, q < (behind(way) + 1) * chunks)
+
+        @pl.when(jnp.logical_and(q >= chunks, q < (behind(way) + 1) * chunks))
+        def _():
+            arrival(way, q - chunks).wait_recv()
+
+        @pl.when(jnp.logical_and(sends, q >= window))
+        def _():
+            send(way, q - window, False).wait_send()
+
+        @pl.when(jnp.logical_and(sends, q < chunks))
+        def _():
+            send(way, q, True).start()
+
+        @pl.when(jnp.logical_and(sends, q >= chunks))
+        def _():
+            send(way, q, False).start()
+
+    @pl.loop(0, teams * chunks)
     def _(q):
-        has_left = q < t * chunks
-        has_right = q < (teams - 1 - t) * chunks
-
-        @pl.when(has_left)
-        def _():
-            arrival(1, q).wait_recv()
-
-            @pl.when(t < teams - 1)
+        forward(1, q)
+        forward(-1, q)
+
+        @pl.when(q < chunks)
+        def _():
+            cov_copy(q).wait()
+            value = stage[span(q), :]
+            top = value.astype(jnp.bfloat16)
+            high[span(q), :] = top
+            low[span(q), :] = (value - top.astype(jnp.float32)).astype(jnp.bfloat16)
+            multiply(t, q)
+
+        for way in (1, -1):
+            @pl.when(jnp.logical_and(q >= chunks, q < (behind(way) + 1) * chunks))
             def _():
-                send(1, q + chunks, False).start()
-
-        @pl.when(has_right)
-        def _():
-            arrival(-1, q).wait_recv()
-
-            @pl.when(t > 0)
-            def _():
-                send(-1, q + chunks, False).start()
-
-        @pl.when(has_left)
-        def _():
-            multiply(t - 1 - q // chunks, lax.rem(q, chunks))
-
-        @pl.when(has_right)
-        def _():
-            multiply(t + 1 + q // chunks, lax.rem(q, chunks))
+                multiply(t - way * (q // chunks), lax.rem(q, chunks))
 
     for s in range(teams):
         values = current[s * rows:(s + 1) * rows, :]
@@ -165,30 +162,26 @@
     for d in range(1, reps):
         exchange(d).wait_send()
 
-    @pl.loop(0, teams * chunks)
-    def _(q):
-        @pl.when(jnp.logical_and(t < teams - 1, q < (t + 1) * chunks))
-        def _():
-            send(1, q, False).wait_send()
-
-        @pl.when(jnp.logical_and(t > 0, q < (teams - t) * chunks))
-        def _():
-            send(-1, q, False).wait_send()
+    for way in (1, -1):
+        for w in range(1, window + 1):
+            @pl.when(behind(-way) > 0)
+            def _():
+                send(way, (behind(way) + 1) * chunks - w, False).wait_send()
 
 
 def per_device(teams, reps, omega_rows, covariance_columns, tile_offsets):
     rows, width = omega_rows.shape
     tile = covariance_columns.shape[1]
     share = rows * teams // reps
-    chunks = max(1, min(32 // teams, width // 256))
+    chunks = max(1, min(16 // teams, width // 256))
     dma = pltpu.SemaphoreType.DMA
     moved = pl.pallas_call(
-        functools.partial(kernel, teams, reps, chunks),
+        functools.partial(kernel, teams, reps, chunks, min(2, chunks)),
         out_shape=jax.ShapeDtypeStruct((share, tile), jnp.float32),
         in_specs=[
             pl.BlockSpec(memory_space=pl.ANY),
             pl.BlockSpec(memory_space=pl.ANY),
-            pl.BlockSpec(memory_space=pltpu.SMEM),
+            pl.BlockSpec(memory_space=pl.ANY),
         ],
         out_specs=pl.BlockSpec(memory_space=pltpu.VMEM),
         scratch_shapes=[
@@ -208,9 +201,11 @@
             dma((teams * chunks,)),
             dma((reps - 1,)),
             dma((reps - 1,)),
+            pltpu.SMEM((1,), jnp.int32),
+            dma,
         ],
         compiler_params=pltpu.CompilerParams(
-            collective_id=0, has_side_effects=True, vmem_limit_bytes=48 * 1024 * 1024),
+            collective_id=0, has_side_effects=True, vmem_limit_bytes=63_000_000),
         cost_estimate=pl.CostEstimate(
             flops=8 * teams * rows * width * tile,
             bytes_accessed=4 * width * (tile + rows * teams), transcendentals=0),

time: 46.4 us -> 48.5 us (1.045)
  Pallas kernels: 43.9 us -> 46.1 us
  local copies, waits for them, and re-layouts: 1.04 us -> 0 us
  other arithmetic: 0.69 us -> 1.4 us
    pallas_call x1, Pallas kernels: 43.9 us -> 46.1 us  [per_device(): pl.pallas_call(functools.partial(kernel, teams, reps, chunks, min(2, chun...]
    unnamed x2 -> x0, local copies, waits for them, and re-layouts: 1.04 us -> none
    select_n x1, other arithmetic: 0.68 us -> 1.39 us  [per_device(): return jnp.where(diagonal, moved, shrunk)]
where the time goes in v2:
time: 48.5 us; the launch traced here: 48.2 us
  Pallas kernels  46.1 us (95%)
  other arithmetic  1.4 us (3%)
  between operations  0.68 us (1%)
    pallas_call x1, Pallas kernels, per_device(): pl.pallas_call(functools.partial(kernel, teams, reps, chunks, min(2, chun...  46.1 us
    select_n x1, other arithmetic, per_device(): return jnp.where(diagonal, moved, shrunk)  1.39 us

profile of v2, /device:TPU:0, one launch (start us, length us, event | category | flops | bytes accessed | tf_op | source)
XLA Modules:
  0.0 48.2 jit_solution(8397696023233141093)
XLA Ops:
  0.7 46.1 %shard_map.37 = f32[16,256]{1,0:T(8,128)} custom-call(f32[16,8192]{1,0:T(8,128)} %omega.1, f32[8192,256]{1,0:T(8,128)} %cov.1, s32[1]{0:T(128)} %copy.4.offset), custom_call_target="tpu_custom_call" | custom-call | flops 1073741824 | bytes 10485760 | tf_op jit(solution)/shard_map/pallas_call | solution.py:178
  46.8 1.4 %multiply_select_fusion = f32[16,256]{1,0:T(8,128)} fusion(f32[16,256]{1,0:T(8,128)} %shard_map.37, s32[256]{0:T(256)S(1)} %iota_add_fusion, s32[16]{0:T(128)S(1)} %iota_add_fusion.1), kind=kLoop, calls=%fused_computation | loop fusion | flops 28672 | bytes 33856 | tf_op jit(solution)/shard_map/jit(_where)/select_n | solution.py:217
  (2 shorter events, 0.0 us)

commit v3 on v2

v3 whole, which is shorter than its diff:
```python
import functools

import jax
import jax.numpy as jnp
from jax import lax
from jax.experimental import pallas as pl
from jax.experimental.pallas import tpu as pltpu
from jax.sharding import PartitionSpec as P

MESH = pl.DeviceIdType.MESH
step_size = 0.5
penalty = 0.1


def kernel(teams, reps, widths, lend, omega, cov, offset, out, gath, stage, high, low, acc,
           current, part, inbox, loan, repaid, reply, note_out, note_in, cov_sem, own_sem,
           right_send, right_recv, left_send, left_recv, sum_send, sum_recv, place, place_sem,
           lend_send, lend_recv):
    t = lax.axis_index("team")
    r = lax.axis_index("rep")
    rows, width = omega.shape
    tile = cov.shape[1]
    chunks = len(widths)
    lent = widths[0]
    share = teams * rows // reps

    def span(c):
        return pl.ds(sum(widths[:c]), widths[c])

    def cov_copy(c):
        return pltpu.make_async_copy(cov.at[span(c), :], stage.at[span(c), :], cov_sem.at[c])

    def behind(way):
        return t if way > 0 else teams - 1 - t

    def ahead(way):
        return behind(-way)

    own_copy = pltpu.make_async_copy(omega, gath.at[t], own_sem)
    own_copy.start()
    place_copy = pltpu.make_async_copy(offset, place, place_sem)
    place_copy.start()
    for c in range(chunks):
        cov_copy(c).start()

    barrier = pltpu.get_barrier_semaphore()

    @pl.when(t > 0)
    def _():
        pl.semaphore_signal(barrier, inc=1, device_id={"team": t - 1}, device_id_type=MESH)

    @pl.when(t < teams - 1)
    def _():
        pl.semaphore_signal(barrier, inc=1, device_id={"team": t + 1}, device_id_type=MESH)

    for d in range(1, reps):
        peer = lax.rem(r + d, reps)
        pl.semaphore_signal(barrier, inc=1, device_id={"rep": peer}, device_id_type=MESH)

    sides = jnp.where(t > 0, 1, 0) + jnp.where(t < teams - 1, 1, 0)
    pl.semaphore_wait(barrier, reps - 1 + sides)

    def send(way, j, c):
        q = j * chunks + c
        sems = (right_send, right_recv) if way > 0 else (left_send, left_recv)
        view = gath.at[t - j * way, :, span(c)]
        return pltpu.make_async_remote_copy(
            src_ref=view, dst_ref=view, send_sem=sems[0].at[q], recv_sem=sems[1].at[q],
            device_id={"team": t + way}, device_id_type=MESH)

    def arrival(way, j, c):
        q = j * chunks + c
        sems = (right_send, right_recv) if way > 0 else (left_send, left_recv)
        view = gath.at[t - (j + 1) * way, :, span(c)]
        return pltpu.make_async_remote_copy(
            src_ref=view, dst_ref=view, send_sem=sems[0].at[q], recv_sem=sems[1].at[q],
            device_id={"team": t - way}, device_id_type=MESH)

    def sends(way, j, c):
        least = 1 if lend and c == 0 else 0
        return jnp.logical_and(ahead(way) > least, j <= behind(way))

    def receives(way, j, c):
        wanted = jnp.logical_and(j >= 1, j <= behind(way))
        if lend and c == 0:
            wanted = jnp.logical_and(wanted, ahead(way) > 0)
        return wanted

    def towards(way, source, target, index):
        return pltpu.make_async_remote_copy(
            src_ref=source, dst_ref=target, send_sem=lend_send.at[index],
            recv_sem=lend_recv.at[index], device_id={"team": t + way}, device_id_type=MESH)

    def loan_copy(way):
        return towards(way, cov.at[pl.ds(0, lent), :], loan, 0)

    def note_copy(way):
        return towards(way, note_out, note_in, 1)

    def reply_copy(way):
        others = pl.ds(0 if way > 0 else rows, (teams - 1) * rows)
        return towards(way, reply.at[others, :], repaid.at[others, :], 2)

    place_copy.wait()
    origin = place[0]
    if lend:
        repaid[...] = jnp.zeros_like(repaid)
        note_out[...] = jnp.full(note_out.shape, origin, jnp.int32).astype(jnp.float32)
        for way in (1, -1):
            @pl.when(ahead(way) == 0)
            def _():
                loan_copy(-way).start()
                note_copy(-way).start()

    acc[...] = jnp.zeros_like(acc)
    current[...] = jnp.zeros_like(current)

    def halves(value):
        top = value.astype(jnp.bfloat16)
        return top, (value - top.astype(jnp.float32)).astype(jnp.bfloat16)

    def product(a, b_high, b_low):
        both = jnp.concatenate(halves(a), axis=0)
        whole = jnp.dot(both, b_high, preferred_element_type=jnp.float32)
        whole = whole + jnp.dot(both, b_low, preferred_element_type=jnp.float32)
        return whole[:a.shape[0]] + whole[a.shape[0]:]

    def found(a, begin, where):
        total = jnp.zeros((a.shape[0], tile), jnp.float32)
        for k in range(a.shape[1] // tile):
            here = jnp.full((a.shape[0], tile), begin + k * tile, jnp.int32)
            total = total + jnp.where(here == where, a[:, k * tile:(k + 1) * tile], 0.0)
        return total

    def combined(values, products, first_row, where, low_col, high_col):
        row_ids = first_row + lax.broadcasted_iota(jnp.int32, values.shape, 0)
        col_ids = where + lax.broadcasted_iota(jnp.int32, values.shape, 1)
        mine = jnp.logical_and(col_ids >= low_col, col_ids < high_col)
        diagonal = jnp.logical_and(row_ids == col_ids, mine)
        safe = jnp.where(diagonal, values, 1.0)
        return values + jnp.where(diagonal, step_size / safe, 0.0) - step_size * products

    def multiply(block, c):
        a = gath[block, :, span(c)]
        place_rows = pl.ds(pl.multiple_of(block * rows, rows), rows)
        acc[place_rows, :] += product(a, high[span(c), :], low[span(c), :])
        current[place_rows, :] += found(a, r * width + sum(widths[:c]), origin)

    own_copy.wait()

    @pl.loop(0, teams)
    def _(j):
        for c in range(chunks):
            for way in (1, -1):
                @pl.when(receives(way, j, c))
                def _():
                    arrival(way, j - 1, c).wait_recv()

                ready = sends(way, j, c)
                if c > 0:
                    ready = jnp.logical_and(ready, j >= 1)

                @pl.when(ready)
                def _():
                    send(way, j, c).start()

            if c == 0:
                @pl.when(j == 0)
                def _():
                    for n in range(1, chunks):
                        for way in (1, -1):
                            @pl.when(sends(way, j, n))
                            def _():
                                send(way, j, n).start()

            @pl.when(j == 0)
            def _():
                cov_copy(c).wait()
                top, rest = halves(stage[span(c), :])
                high[span(c), :] = top
                low[span(c), :] = rest
                multiply(t, c)

            for way in (1, -1):
                @pl.when(receives(way, j, c))
                def _():
                    multiply(t - way * j, c)

    if lend:
        for way in (1, -1):
            @pl.when(ahead(way) == 1)
            def _():
                loan_copy(-way).wait_recv()
                note_copy(-way).wait_recv()
                where = note_in[0:1, :].astype(jnp.int32)
                top, rest = halves(loan[...])
                for n in range(teams - 1):
                    block = n if way > 0 else n + 1
                    a = gath[block, :, span(0)]
                    reply[block * rows:(block + 1) * rows, :] = combined(
                        found(a, r * width, where), product(a, top, rest), block * rows, where,
                        r * width, r * width + lent)
                reply_copy(way).start()

    is_end = jnp.logical_or(t == 0, t == teams - 1)
    for s in range(teams):
        low_col = r * width
        if lend:
            low_col = low_col + jnp.where(jnp.logical_and(is_end, t != s), lent, 0)
        block = slice(s * rows, (s + 1) * rows)
        part[block, :] = combined(
            current[block, :], acc[block, :], s * rows, origin, low_col, (r + 1) * width)

    if lend:
        for way in (1, -1):
            @pl.when(ahead(way) == 0)
            def _():
                reply_copy(-way).wait_recv()
                part[...] += repaid[...]

    def exchange(d):
        peer = lax.rem(r + d, reps)
        return pltpu.make_async_remote_copy(
            src_ref=part.at[pl.ds(pl.multiple_of(peer * share, share), share), :],
            dst_ref=inbox.at[d - 1], send_sem=sum_send.at[d - 1], recv_sem=sum_recv.at[d - 1],
            device_id={"rep": peer}, device_id_type=MESH)

    for d in range(1, reps):
        exchange(d).start()
    total = part[pl.ds(pl.multiple_of(r * share, share), share), :]
    for d in range(1, reps):
        exchange(d).wait_recv()
        total = total + inbox[d - 1]
    out[...] = total

    for d in range(1, reps):
        exchange(d).wait_send()

    for way in (1, -1):
        if lend:
            @pl.when(ahead(way) == 0)
            def _():
                loan_copy(-way).wait_send()
                note_copy(-way).wait_send()

            @pl.when(ahead(way) == 1)
            def _():
                reply_copy(way).wait_send()

        @pl.loop(0, teams)
        def _(j):
            for c in range(chunks):
                @pl.when(sends(way, j, c))
                def _():
                    send(way, j, c).wait_send()


def per_device(teams, reps, omega_rows, covariance_columns, tile_offsets):
    rows, width = omega_rows.shape
    tile = covariance_columns.shape[1]
    share = rows * teams // reps
    units = width // tile
    lend = teams >= 4 and units >= 8
    exact = units * (teams - 2) * rows // ((teams - 1) * rows + tile)
    lent = max(1, min(exact, units // 8))
    long = max(1, (units - lent) * 3 // 7)
    widths = [n * tile for n in (lent, long, long, units - lent - 2 * long)]
    chunks = len(widths)
    dma = pltpu.SemaphoreType.DMA
    moved = pl.pallas_call(
        functools.partial(kernel, teams, reps, widths, lend),
        out_shape=jax.ShapeDtypeStruct((share, tile), jnp.float32),
        in_specs=[
            pl.BlockSpec(memory_space=pl.ANY),
            pl.BlockSpec(memory_space=pl.ANY),
            pl.BlockSpec(memory_space=pl.ANY),
        ],
        out_specs=pl.BlockSpec(memory_space=pltpu.VMEM),
        scratch_shapes=[
            pltpu.VMEM((teams, rows, width), jnp.float32),
            pltpu.VMEM((width, tile), jnp.float32),
            pltpu.VMEM((width, tile), jnp.bfloat16),
            pltpu.VMEM((width, tile), jnp.bfloat16),
            pltpu.VMEM((teams * rows, tile), jnp.float32),
            pltpu.VMEM((teams * rows, tile), jnp.float32),
            pltpu.VMEM((teams * rows, tile), jnp.float32),
            pltpu.VMEM((reps - 1, share, tile), jnp.float32),
            pltpu.VMEM((widths[0], tile), jnp.float32),
            pltpu.VMEM((teams * rows, tile), jnp.float32),
            pltpu.VMEM((teams * rows, tile), jnp.float32),
            pltpu.VMEM((8, tile), jnp.float32),
            pltpu.VMEM((8, tile), jnp.float32),
            dma((chunks,)),
            dma,
            dma((teams * chunks,)),
            dma((teams * chunks,)),
            dma((teams * chunks,)),
            dma((teams * chunks,)),
            dma((reps - 1,)),
            dma((reps - 1,)),
            pltpu.SMEM((1,), jnp.int32),
            dma,
            dma((3,)),
            dma((3,)),
        ],
        compiler_params=pltpu.CompilerParams(
            collective_id=0, has_side_effects=True, vmem_limit_bytes=50_000_000),
        cost_estimate=pl.CostEstimate(
            flops=8 * teams * rows * width * tile,
            bytes_accessed=4 * width * (tile + rows * teams), transcendentals=0),
    )(omega_rows, covariance_columns, tile_offsets)
    global_rows = lax.axis_index("rep") * share + jnp.arange(share, dtype=jnp.int32)
    global_cols = tile_offsets[0] + jnp.arange(tile, dtype=jnp.int32)
    diagonal = global_rows[:, None] == global_cols[None, :]
    shrunk = jnp.sign(moved) * jnp.maximum(jnp.abs(moved) - step_size * penalty, 0.0)
    return jnp.where(diagonal, moved, shrunk)


def solution(mesh):
    in_specs = (P(("groups", "team"), "rep"), P("rep", ("groups", "team")), P(("groups", "team")))
    out_specs = P("rep", ("groups", "team"))
    body = functools.partial(per_device, mesh.shape["team"], mesh.shape["rep"])
    return jax.shard_map(body, mesh=mesh, in_specs=in_specs, out_specs=out_specs, check_vma=False)
```

time: 48.5 us -> 56.7 us (1.17)
  Pallas kernels: 46.1 us -> 54.1 us
  local copies, waits for them, and re-layouts: 0 us -> 1.04 us
  other arithmetic: 1.4 us -> 0.69 us
    pallas_call x1, Pallas kernels: 46.1 us -> 54.1 us  [per_device(): pl.pallas_call(functools.partial(kernel, teams, reps, widths, lend), out_...]
    unnamed x0 -> x2, local copies, waits for them, and re-layouts: none -> 1.04 us
    select_n x1, other arithmetic: 1.39 us -> 0.68 us  [per_device(): return jnp.where(diagonal, moved, shrunk)]
where the time goes in v3:
time: 56.7 us; the launch traced here: 56.5 us
  Pallas kernels  54.1 us (95%)
  local copies, waits for them, and re-layouts  1.04 us (2%)
  other arithmetic  0.69 us (1%)
  between operations  0.68 us (1%)
    pallas_call x1, Pallas kernels, per_device(): pl.pallas_call(functools.partial(kernel, teams, reps, widths, lend), out_...  54.1 us

profile of v3, /device:TPU:0, one launch (start us, length us, event | category | flops | bytes accessed | tf_op | source)
XLA Modules:
  0.0 56.5 jit_solution(6769879573152162375)
XLA Ops:
  0.7 0.0 copy-start
  0.7 1.0 %copy-done = f32[16,8192]{1,0:T(8,128)S(1)} copy-done((f32[16,8192]{1,0:T(8,128)S(1)}, f32[16,8192]{1,0:T(8,128)}, u32[]{:S(2)}) %copy-start) | copy-done | bytes 524312
  1.7 54.1 %shard_map.37 = f32[16,256]{1,0:T(8,128)S(1)} custom-call(f32[16,8192]{1,0:T(8,128)S(1)} %copy-done, f32[8192,256]{1,0:T(8,128)} %cov.1, s32[1]{0:T(128)} %copy.4.offset), custom_call_target="tpu_custom_call" | custom-call | flops 1073741824 | bytes 10485760 | tf_op jit(solution)/shard_map/pallas_call | solution.py:270
  55.8 0.7 %multiply_select_fusion = f32[16,256]{1,0:T(8,128)} fusion(f32[16,256]{1,0:T(8,128)S(1)} %shard_map.37, s32[256]{0:T(256)S(1)} %iota_add_fusion, s32[16]{0:T(128)S(1)} %iota_add_fusion.1), kind=kLoop, calls=%fused_computation | loop fusion | flops 28672 | bytes 33856 | tf_op jit(solution)/shard_map/jit(_where)/select_n | solution.py:316
  (2 shorter events, 0.0 us)
Async XLA Ops:
  0.7 1.0 %copy-start = (f32[16,8192]{1,0:T(8,128)S(1)}, f32[16,8192]{1,0:T(8,128)}, u32[]{:S(2)}) copy-start(f32[16,8192]{1,0:T(8,128)} %omega.1) | copy-start | bytes 1572868

commit v4 on v3

--- a/solution.py
+++ b/solution.py
@@ -106,11 +106,6 @@
     if lend:
         repaid[...] = jnp.zeros_like(repaid)
         note_out[...] = jnp.full(note_out.shape, origin, jnp.int32).astype(jnp.float32)
-        for way in (1, -1):
-            @pl.when(ahead(way) == 0)
-            def _():
-                loan_copy(-way).start()
-                note_copy(-way).start()
 
     acc[...] = jnp.zeros_like(acc)
     current[...] = jnp.zeros_like(current)
@@ -172,6 +167,15 @@
                             @pl.when(sends(way, j, n))
                             def _():
                                 send(way, j, n).start()
+
+            if lend and c == 0:
+                @pl.when(j == 0)
+                def _():
+                    for way in (1, -1):
+                        @pl.when(ahead(way) == 0)
+                        def _():
+                            loan_copy(-way).start()
+                            note_copy(-way).start()
 
             @pl.when(j == 0)
             def _():

time: 56.7 us -> 43.3 us (0.76)
  Pallas kernels: 54.1 us -> 40.8 us
    pallas_call x1, Pallas kernels: 54.1 us -> 40.8 us  [per_device(): pl.pallas_call(functools.partial(kernel, teams, reps, widths, lend), out_...]
where the time goes in v4:
time: 43.3 us; the launch traced here: 43.2 us
  Pallas kernels  40.8 us (94%)
  local copies, waits for them, and re-layouts  1.04 us (2%)
  other arithmetic  0.69 us (2%)
  between operations  0.68 us (2%)
    pallas_call x1, Pallas kernels, per_device(): pl.pallas_call(functools.partial(kernel, teams, reps, widths, lend), out_...  40.8 us
    unnamed x2, local copies, waits for them, and re-layouts  1.04 us

profile of v4, /device:TPU:0, one launch (start us, length us, event | category | flops | bytes accessed | tf_op | source)
XLA Modules:
  0.0 43.2 jit_solution(16015139833487606233)
XLA Ops:
  0.7 0.0 copy-start
  0.7 1.0 %copy-done = f32[16,8192]{1,0:T(8,128)S(1)} copy-done((f32[16,8192]{1,0:T(8,128)S(1)}, f32[16,8192]{1,0:T(8,128)}, u32[]{:S(2)}) %copy-start) | copy-done | bytes 524312
  1.7 40.8 %shard_map.37 = f32[16,256]{1,0:T(8,128)S(1)} custom-call(f32[16,8192]{1,0:T(8,128)S(1)} %copy-done, f32[8192,256]{1,0:T(8,128)} %cov.1, s32[1]{0:T(128)} %copy.4.offset), custom_call_target="tpu_custom_call" | custom-call | flops 1073741824 | bytes 10485760 | tf_op jit(solution)/shard_map/pallas_call | solution.py:274
  42.5 0.7 %multiply_select_fusion = f32[16,256]{1,0:T(8,128)} fusion(f32[16,256]{1,0:T(8,128)S(1)} %shard_map.37, s32[256]{0:T(256)S(1)} %iota_add_fusion, s32[16]{0:T(128)S(1)} %iota_add_fusion.1), kind=kLoop, calls=%fused_computation | loop fusion | flops 28672 | bytes 33856 | tf_op jit(solution)/shard_map/jit(_where)/select_n | solution.py:320
  (2 shorter events, 0.0 us)
Async XLA Ops:
  0.7 1.0 %copy-start = (f32[16,8192]{1,0:T(8,128)S(1)}, f32[16,8192]{1,0:T(8,128)}, u32[]{:S(2)}) copy-start(f32[16,8192]{1,0:T(8,128)} %omega.1) | copy-start | bytes 1572868
